TPU v7x, 32 devices: a whole 2x2x4 slice. The times are simulated.
32 devices in a mesh: gx: 4 (over y, x), gy: 8 (over z, core).
Axes of the slice: x: 2, y: 2, z: 4, core: 2. Of those that a mesh axis runs over, the one named last changes fastest.
Arguments:
- pulses_in: float32 [12, 64, 128, 256], P(None, 'gx', 'gy'), may hold values from -6 to 6
- node_loss: float32 [64, 128, 256], P('gx', 'gy'), may hold values from 0.5 to 1
- surface_cells: int32 [4, 8, 512], P('gx', 'gy'), may hold values from 0 to 65535
- surface_normal: int32 [4, 8, 512], P('gx', 'gy'), may hold values from 0 to 6, as said below
- owner_dirs: int32 [4096], replicated, may hold values from 0 to 4095, each once
Outputs:
- pulses_out: float32 [12, 64, 128, 256], P(None, 'gx', 'gy')
- far_field: float32 [4096, 96], P(('gx', 'gy'))
Inputs may be any that keep to these rules, and one draw needn't show every extreme that they name: `surface_normal`: on each device the live slots (codes 1 to 6: outward normal +x, -x, +y, -y, +z, -z) come first and the rest are 0; at most 512 are live on a device and some device has all 512 live.
All inputs are finite; a program needn't handle non-finite values.
Results may differ from a plain program's by a relative error of at most 0.0003.
Values sent between devices are 32-bit elements; how exact they have to be, the bound alone decides.
A program may use at most 128 MiB of HBM per device.

v0:
```python
import math

import jax
import jax.numpy as jnp
import numpy as np
from jax import lax
from jax.sharding import PartitionSpec as P

DIRS = 4096
FREQ = 8


HIGH = lax.Precision.HIGHEST
OTHERS = ((1, 2), (0, 2), (0, 1))


def shifted(block, axis, distance):
    devices = range(lax.axis_size(axis))
    route = [(i - distance, i) for i in devices if i - distance in devices]
    return lax.ppermute(block, axis, route)


def port_of(arm_axis, arm_sign, polarity):
    return 4 * arm_axis + (0 if arm_sign > 0 else 2) + OTHERS[arm_axis].index(polarity)


def node_tables():
    scatter_table = np.zeros((12, 12))
    field_table = np.zeros((6, 12))
    for arm_axis in range(3):
        for arm_sign in (1, -1):
            for polarity in OTHERS[arm_axis]:
                port_k = port_of(arm_axis, arm_sign, polarity)
                third_axis = 3 - arm_axis - polarity
                scatter_table[port_k, port_of(third_axis, 1, polarity)] += 0.5
                scatter_table[port_k, port_of(third_axis, -1, polarity)] += 0.5
                scatter_table[port_k, port_of(polarity, -1, arm_axis)] += 0.5 * arm_sign
                scatter_table[port_k, port_of(polarity, 1, arm_axis)] -= 0.5 * arm_sign
                field_table[polarity, port_k] += 0.5
    for third_axis in range(3):
        first_axis, second_axis = OTHERS[third_axis]
        field_table[3 + third_axis, port_of(first_axis, 1, second_axis)] += 0.5
        field_table[3 + third_axis, port_of(first_axis, -1, second_axis)] -= 0.5
        field_table[3 + third_axis, port_of(second_axis, 1, first_axis)] -= 0.5
        field_table[3 + third_axis, port_of(second_axis, -1, first_axis)] += 0.5
    return (scatter_table.astype(np.float32), field_table.astype(np.float32))


def scatter_node(incident, node_loss):
    scatter_table = jnp.asarray(node_tables()[0])
    return node_loss[None] * jnp.einsum("kl,lxyz->kxyz", scatter_table, incident, precision=HIGH)


def connect_tile(reflected):
    zero_plane = jnp.zeros_like(reflected[8:10, :, :, :1])
    plus_z = jnp.concatenate([reflected[10:12, :, :, 1:], zero_plane], axis=3)
    minus_z = jnp.concatenate([zero_plane, reflected[8:10, :, :, :-1]], axis=3)
    from_next_x = shifted(reflected[2:4, :1], "gx", -1)
    from_prev_x = shifted(reflected[0:2, -1:], "gx", 1)
    from_next_y = shifted(reflected[6:8, :, :1], "gy", -1)
    from_prev_y = shifted(reflected[4:6, :, -1:], "gy", 1)
    plus_x = jnp.concatenate([reflected[2:4, 1:], from_next_x], axis=1)
    minus_x = jnp.concatenate([from_prev_x, reflected[0:2, :-1]], axis=1)
    plus_y = jnp.concatenate([reflected[6:8, :, 1:], from_next_y], axis=2)
    minus_y = jnp.concatenate([from_prev_y, reflected[4:6, :, :-1]], axis=2)
    return jnp.concatenate([plus_x, minus_x, plus_y, minus_y, plus_z, minus_z], axis=0)


def cross_three(left, right):
    return jnp.stack(
        [
            left[1] * right[2] - left[2] * right[1],
            left[2] * right[0] - left[0] * right[2],
            left[0] * right[1] - left[1] * right[0],
        ]
    )


def surface_currents(slot_pulses, normal_code):
    field_table = jnp.asarray(node_tables()[1])
    fields = jnp.dot(field_table, slot_pulses, precision=HIGH)
    live = normal_code > 0
    normal_axis = (normal_code - 1) // 2
    outward = 1.0 - 2.0 * ((normal_code - 1) % 2).astype(jnp.float32)
    normal = jnp.stack(
        [jnp.where(live & (normal_axis == which), outward, 0.0) for which in range(3)]
    )
    return jnp.concatenate(
        [cross_three(normal, fields[3:6]), -cross_three(normal, fields[0:3])], axis=0
    )


def unit_vectors(direction_ids):
    theta_count = DIRS // 64
    theta = math.pi * ((direction_ids // 64).astype(jnp.float32) + 0.5) / theta_count
    azimuth = 2.0 * math.pi * (direction_ids % 64).astype(jnp.float32) / 64.0
    return jnp.stack(
        [jnp.sin(theta) * jnp.cos(azimuth), jnp.sin(theta) * jnp.sin(azimuth), jnp.cos(theta)],
        axis=1,
    )


def far_term(direction_ids, slot_data, positions, scale):
    units = unit_vectors(direction_ids)
    projected = jnp.dot(units, positions, precision=HIGH)
    first = slot_data[0:6]
    second = slot_data[6:12]

    def one_freq(f_index):
        omega = 2.0 * math.pi * (f_index + 1.0) / 64.0
        real_part = first * jnp.cos(omega) + second * jnp.cos(2.0 * omega)
        imag_part = -(first * jnp.sin(omega) + second * jnp.sin(2.0 * omega))
        phase_angle = 2.0 * omega * projected
        upper = jnp.concatenate([real_part, imag_part], axis=0)
        lower = jnp.concatenate([-imag_part, real_part], axis=0)
        return jnp.einsum("nm,cm->nc", jnp.cos(phase_angle), upper, precision=HIGH) + jnp.einsum(
            "nm,cm->nc", jnp.sin(phase_angle), lower, precision=HIGH
        )

    per_freq = lax.map(one_freq, jnp.arange(FREQ, dtype=jnp.float32))
    rows_here = direction_ids.shape[0]
    return jnp.transpose(per_freq, (1, 0, 2)).reshape(rows_here, FREQ * 12) * scale


def per_device(pulses_in, node_loss, surface_cells, surface_normal, owner_dirs):
    tile_x = pulses_in.shape[1]
    tile_y = pulses_in.shape[2]
    tile_z = pulses_in.shape[3]
    slot_count = surface_cells.shape[2]
    size_x = lax.axis_size("gx")
    size_y = lax.axis_size("gy")
    incident_one = connect_tile(scatter_node(pulses_in, node_loss))
    incident_two = connect_tile(scatter_node(incident_one, node_loss))
    cell_index = surface_cells[0, 0]
    codes = surface_normal[0, 0]
    slots_one = jnp.take(incident_one.reshape(12, -1), cell_index, axis=1)
    slots_two = jnp.take(incident_two.reshape(12, -1), cell_index, axis=1)
    slot_data = jnp.concatenate(
        [surface_currents(slots_one, codes), surface_currents(slots_two, codes)], axis=0
    )
    x_cell = lax.axis_index("gx") * tile_x + cell_index // (tile_y * tile_z)
    y_cell = lax.axis_index("gy") * tile_y + cell_index // tile_z % tile_y
    z_cell = cell_index % tile_z
    positions = jnp.stack(
        [
            x_cell.astype(jnp.float32) - (tile_x * size_x - 1) / 2.0,
            y_cell.astype(jnp.float32) - (tile_y * size_y - 1) / 2.0,
            z_cell.astype(jnp.float32) - (tile_z - 1) / 2.0,
        ]
    )
    scale = 1.0 / math.sqrt(size_x * size_y * slot_count)
    far_field = lax.psum_scatter(
        far_term(owner_dirs, slot_data, positions, scale),
        ("gx", "gy"),
        scatter_dimension=0,
        tiled=True,
    )
    return (incident_two, far_field)


def solution(mesh):
    return jax.shard_map(
        per_device,
        mesh=mesh,
        in_specs=(
            P(None, "gx", "gy", None),
            P("gx", "gy", None),
            P("gx", "gy", None),
            P("gx", "gy", None),
            P(),
        ),
        out_specs=(P(None, "gx", "gy", None), P(("gx", "gy"), None)),
        check_vma=False,
    )
```

profile of v0, /device:TPU:0, one launch (start us, length us, event | category | flops | bytes accessed | tf_op | source)
XLA Modules:
  0.0 848.2 jit_solution(134801786795019936)
XLA Ops:
  9.1 6.5 fusion.27
  15.6 2.4 collective-permute-start.3
  19.3 4.2 collective-permute-start.1
  27.7 9.0 %fusion.40 = f32[4096,512]{1,0:T(8,128)} fusion(f32[4096,1]{0,1:T(1,128)S(1)} %bitcast.93, f32[4096,1]{0,1:T(1,128)S(1)} %bitcast.92, f32[4096,1]{0,1:T(1,128)S(1)} %bitcast.91, f32[1,512]{1,0:T(1,128)S(1)} %fusion.65, f32[1,512]{1,0:T(1,128)S(1)} %get-tuple-element.152, f32[1,512]{1,0:T(1,128)S(1)} %get-tuple-element.192), kind=kOutput, calls=%fused_computation.46 | convolution fusion | flops 75525120 | bytes 8443904 | tf_op jit(solution)/shard_map/dot_general | solution.py:105
  39.9 7.3 concatenate.72
  47.3 5.5 multiply_bitcast_fusion
  55.2 18.5 %copy.20 = f32[12,16,16,256]{0,3,2,1:T(8,128)} copy(f32[12,16,16,256]{3,0,2,1:T(8,128)} %concatenate.72) | data formatting | bytes 6291456 | tf_op jit(solution)/shard_map/reshape | solution.py:136
  73.7 4.1 collective-permute-start.7
  79.1 4.3 collective-permute-start.5
  84.9 11.6 %gather_fusion = f32[512,12]{1,0:T(8,128)S(1)} fusion(f32[12,65536]{0,1:T(8,128)} %bitcast.89, s32[1024]{0:T(1024)S(1)} %pad_clamp_fusion), kind=kCustom, calls=%fused_computation.clone | custom fusion | bytes 51200 | tf_op jit(solution)/shard_map/jit(_take)/gather | solution.py:136
  100.1 7.3 concatenate.79
  107.5 18.5 %copy.21 = f32[12,16,16,256]{0,3,2,1:T(8,128)} copy(f32[12,16,16,256]{3,0,2,1:T(8,128)} %concatenate.79) | data formatting | bytes 6291456 | tf_op jit(solution)/shard_map/reshape | solution.py:137
  126.0 11.6 %gather_fusion.1 = f32[512,12]{1,0:T(8,128)S(1)} fusion(f32[12,65536]{0,1:T(8,128)} %bitcast.90, s32[1024]{0:T(1024)S(1)} %pad_clamp_fusion), kind=kCustom, calls=%fused_computation.1.clone | custom fusion | bytes 51200 | tf_op jit(solution)/shard_map/jit(_take)/gather | solution.py:137
  138.2 596.6 %while.14 = (s32[]{:T(128)}, f32[8,4096,12]{1,2,0:T(8,128)}, f32[8]{0:T(128)S(1)}, f32[4096,512]{1,0:T(8,128)}, f32[6,512]{1,0:T(8,128)S(1)}, /*index=5*/f32[6,5...) while((s32[]{:T(128)}, f32[8,4096,12]{1,2,0:T(8,128)}, f32[8]{0:T(128)S(1)}, ...), condition=%wide.region_1.3_spmd, body=%wide.region_0.0_spmd.sunk | while | flops 608257024 | bytes 51098852 | solution.py:120
  139.9 37.4 %fusion.107 = f32[4096,12]{0,1:T(8,128)S(1)} fusion(f32[4096,512]{1,0:T(8,128)} %get-tuple-element.261, f32[]{:T(128)} %bitcast.86, f32[6,512]{1,0:T(8,128)S(1)} %get-tuple-element.235, f32[6,512]{1,0:T(8,128)S(1)} %get-tuple-element.236), kind=kOutput, calls=%fused_computation.2.clone.1 | convolution fusion | flops 304093184 | bytes 8609796 | tf_op jit(solution)/shard_map/while/body/eval_jaxpr/nm,cm->nc/dot_general | solution.py:116
  177.3 35.5 %fusion.108 = f32[8,4096,12]{1,2,0:T(8,128)} fusion(f32[8,4096,12]{1,2,0:T(8,128)} %get-tuple-element.249, s32[]{:T(128)} %get-tuple-element.248, f32[4096,12]{0,1:T(8,128)S(1)} %fusion.107, f32[4096,512]{1,0:T(8,128)S(1)} %copy-done.2, f32[]{:T(128)} %bitcast.86, f32[6,512]{1,0:T(8,128)S(1)} %get-tuple-element.237, f32[6,512]{1,0:T(8,128)S(1)} %get-tuple-element.235), kind=kOutput, calls=%fused_computation.10.clone.1 | convolution fusion | flops 304142336 | bytes 8872960 | tf_op jit(solution)/shard_map/while/body/eval_jaxpr/nm,cm->nc/dot_general | solution.py:116
  214.4 37.4 %fusion.107 = f32[4096,12]{0,1:T(8,128)S(1)} fusion(f32[4096,512]{1,0:T(8,128)} %get-tuple-element.261, f32[]{:T(128)} %bitcast.86, f32[6,512]{1,0:T(8,128)S(1)} %get-tuple-element.235, f32[6,512]{1,0:T(8,128)S(1)} %get-tuple-element.236), kind=kOutput, calls=%fused_computation.2.clone.1 | convolution fusion | flops 304093184 | bytes 8609796 | tf_op jit(solution)/shard_map/while/body/eval_jaxpr/nm,cm->nc/dot_general | solution.py:116
  251.9 35.5 %fusion.108 = f32[8,4096,12]{1,2,0:T(8,128)} fusion(f32[8,4096,12]{1,2,0:T(8,128)} %get-tuple-element.249, s32[]{:T(128)} %get-tuple-element.248, f32[4096,12]{0,1:T(8,128)S(1)} %fusion.107, f32[4096,512]{1,0:T(8,128)S(1)} %copy-done.2, f32[]{:T(128)} %bitcast.86, f32[6,512]{1,0:T(8,128)S(1)} %get-tuple-element.237, f32[6,512]{1,0:T(8,128)S(1)} %get-tuple-element.235), kind=kOutput, calls=%fused_computation.10.clone.1 | convolution fusion | flops 304142336 | bytes 8872960 | tf_op jit(solution)/shard_map/while/body/eval_jaxpr/nm,cm->nc/dot_general | solution.py:116
  289.0 37.4 %fusion.107 = f32[4096,12]{0,1:T(8,128)S(1)} fusion(f32[4096,512]{1,0:T(8,128)} %get-tuple-element.261, f32[]{:T(128)} %bitcast.86, f32[6,512]{1,0:T(8,128)S(1)} %get-tuple-element.235, f32[6,512]{1,0:T(8,128)S(1)} %get-tuple-element.236), kind=kOutput, calls=%fused_computation.2.clone.1 | convolution fusion | flops 304093184 | bytes 8609796 | tf_op jit(solution)/shard_map/while/body/eval_jaxpr/nm,cm->nc/dot_general | solution.py:116
  326.4 35.5 %fusion.108 = f32[8,4096,12]{1,2,0:T(8,128)} fusion(f32[8,4096,12]{1,2,0:T(8,128)} %get-tuple-element.249, s32[]{:T(128)} %get-tuple-element.248, f32[4096,12]{0,1:T(8,128)S(1)} %fusion.107, f32[4096,512]{1,0:T(8,128)S(1)} %copy-done.2, f32[]{:T(128)} %bitcast.86, f32[6,512]{1,0:T(8,128)S(1)} %get-tuple-element.237, f32[6,512]{1,0:T(8,128)S(1)} %get-tuple-element.235), kind=kOutput, calls=%fused_computation.10.clone.1 | convolution fusion | flops 304142336 | bytes 8872960 | tf_op jit(solution)/shard_map/while/body/eval_jaxpr/nm,cm->nc/dot_general | solution.py:116
  363.6 37.4 %fusion.107 = f32[4096,12]{0,1:T(8,128)S(1)} fusion(f32[4096,512]{1,0:T(8,128)} %get-tuple-element.261, f32[]{:T(128)} %bitcast.86, f32[6,512]{1,0:T(8,128)S(1)} %get-tuple-element.235, f32[6,512]{1,0:T(8,128)S(1)} %get-tuple-element.236), kind=kOutput, calls=%fused_computation.2.clone.1 | convolution fusion | flops 304093184 | bytes 8609796 | tf_op jit(solution)/shard_map/while/body/eval_jaxpr/nm,cm->nc/dot_general | solution.py:116
  401.0 35.5 %fusion.108 = f32[8,4096,12]{1,2,0:T(8,128)} fusion(f32[8,4096,12]{1,2,0:T(8,128)} %get-tuple-element.249, s32[]{:T(128)} %get-tuple-element.248, f32[4096,12]{0,1:T(8,128)S(1)} %fusion.107, f32[4096,512]{1,0:T(8,128)S(1)} %copy-done.2, f32[]{:T(128)} %bitcast.86, f32[6,512]{1,0:T(8,128)S(1)} %get-tuple-element.237, f32[6,512]{1,0:T(8,128)S(1)} %get-tuple-element.235), kind=kOutput, calls=%fused_computation.10.clone.1 | convolution fusion | flops 304142336 | bytes 8872960 | tf_op jit(solution)/shard_map/while/body/eval_jaxpr/nm,cm->nc/dot_general | solution.py:116
  438.1 37.4 %fusion.107 = f32[4096,12]{0,1:T(8,128)S(1)} fusion(f32[4096,512]{1,0:T(8,128)} %get-tuple-element.261, f32[]{:T(128)} %bitcast.86, f32[6,512]{1,0:T(8,128)S(1)} %get-tuple-element.235, f32[6,512]{1,0:T(8,128)S(1)} %get-tuple-element.236), kind=kOutput, calls=%fused_computation.2.clone.1 | convolution fusion | flops 304093184 | bytes 8609796 | tf_op jit(solution)/shard_map/while/body/eval_jaxpr/nm,cm->nc/dot_general | solution.py:116
  475.6 35.5 %fusion.108 = f32[8,4096,12]{1,2,0:T(8,128)} fusion(f32[8,4096,12]{1,2,0:T(8,128)} %get-tuple-element.249, s32[]{:T(128)} %get-tuple-element.248, f32[4096,12]{0,1:T(8,128)S(1)} %fusion.107, f32[4096,512]{1,0:T(8,128)S(1)} %copy-done.2, f32[]{:T(128)} %bitcast.86, f32[6,512]{1,0:T(8,128)S(1)} %get-tuple-element.237, f32[6,512]{1,0:T(8,128)S(1)} %get-tuple-element.235), kind=kOutput, calls=%fused_computation.10.clone.1 | convolution fusion | flops 304142336 | bytes 8872960 | tf_op jit(solution)/shard_map/while/body/eval_jaxpr/nm,cm->nc/dot_general | solution.py:116
  512.7 37.4 %fusion.107 = f32[4096,12]{0,1:T(8,128)S(1)} fusion(f32[4096,512]{1,0:T(8,128)} %get-tuple-element.261, f32[]{:T(128)} %bitcast.86, f32[6,512]{1,0:T(8,128)S(1)} %get-tuple-element.235, f32[6,512]{1,0:T(8,128)S(1)} %get-tuple-element.236), kind=kOutput, calls=%fused_computation.2.clone.1 | convolution fusion | flops 304093184 | bytes 8609796 | tf_op jit(solution)/shard_map/while/body/eval_jaxpr/nm,cm->nc/dot_general | solution.py:116
  550.1 35.5 %fusion.108 = f32[8,4096,12]{1,2,0:T(8,128)} fusion(f32[8,4096,12]{1,2,0:T(8,128)} %get-tuple-element.249, s32[]{:T(128)} %get-tuple-element.248, f32[4096,12]{0,1:T(8,128)S(1)} %fusion.107, f32[4096,512]{1,0:T(8,128)S(1)} %copy-done.2, f32[]{:T(128)} %bitcast.86, f32[6,512]{1,0:T(8,128)S(1)} %get-tuple-element.237, f32[6,512]{1,0:T(8,128)S(1)} %get-tuple-element.235), kind=kOutput, calls=%fused_computation.10.clone.1 | convolution fusion | flops 304142336 | bytes 8872960 | tf_op jit(solution)/shard_map/while/body/eval_jaxpr/nm,cm->nc/dot_general | solution.py:116
  587.3 37.4 %fusion.107 = f32[4096,12]{0,1:T(8,128)S(1)} fusion(f32[4096,512]{1,0:T(8,128)} %get-tuple-element.261, f32[]{:T(128)} %bitcast.86, f32[6,512]{1,0:T(8,128)S(1)} %get-tuple-element.235, f32[6,512]{1,0:T(8,128)S(1)} %get-tuple-element.236), kind=kOutput, calls=%fused_computation.2.clone.1 | convolution fusion | flops 304093184 | bytes 8609796 | tf_op jit(solution)/shard_map/while/body/eval_jaxpr/nm,cm->nc/dot_general | solution.py:116
  624.7 35.5 %fusion.108 = f32[8,4096,12]{1,2,0:T(8,128)} fusion(f32[8,4096,12]{1,2,0:T(8,128)} %get-tuple-element.249, s32[]{:T(128)} %get-tuple-element.248, f32[4096,12]{0,1:T(8,128)S(1)} %fusion.107, f32[4096,512]{1,0:T(8,128)S(1)} %copy-done.2, f32[]{:T(128)} %bitcast.86, f32[6,512]{1,0:T(8,128)S(1)} %get-tuple-element.237, f32[6,512]{1,0:T(8,128)S(1)} %get-tuple-element.235), kind=kOutput, calls=%fused_computation.10.clone.1 | convolution fusion | flops 304142336 | bytes 8872960 | tf_op jit(solution)/shard_map/while/body/eval_jaxpr/nm,cm->nc/dot_general | solution.py:116
  661.8 37.4 %fusion.107 = f32[4096,12]{0,1:T(8,128)S(1)} fusion(f32[4096,512]{1,0:T(8,128)} %get-tuple-element.261, f32[]{:T(128)} %bitcast.86, f32[6,512]{1,0:T(8,128)S(1)} %get-tuple-element.235, f32[6,512]{1,0:T(8,128)S(1)} %get-tuple-element.236), kind=kOutput, calls=%fused_computation.2.clone.1 | convolution fusion | flops 304093184 | bytes 8609796 | tf_op jit(solution)/shard_map/while/body/eval_jaxpr/nm,cm->nc/dot_general | solution.py:116
  699.3 35.5 %fusion.108 = f32[8,4096,12]{1,2,0:T(8,128)} fusion(f32[8,4096,12]{1,2,0:T(8,128)} %get-tuple-element.249, s32[]{:T(128)} %get-tuple-element.248, f32[4096,12]{0,1:T(8,128)S(1)} %fusion.107, f32[4096,512]{1,0:T(8,128)S(1)} %copy-done.2, f32[]{:T(128)} %bitcast.86, f32[6,512]{1,0:T(8,128)S(1)} %get-tuple-element.237, f32[6,512]{1,0:T(8,128)S(1)} %get-tuple-element.235), kind=kOutput, calls=%fused_computation.10.clone.1 | convolution fusion | flops 304142336 | bytes 8872960 | tf_op jit(solution)/shard_map/while/body/eval_jaxpr/nm,cm->nc/dot_general | solution.py:116
  737.9 5.8 copy.18
  743.7 97.6 %reduce-scatter.2.cloned.1.call-done = f32[128,96]{0,1:T(8,128)} async-done(((f32[4096,96]{0,1:T(8,128)}), f32[128,96]{0,1:T(8,128)}) %reduce-scatter.2.cloned.1.call-update) | async-done | bytes 49168 | tf_op jit(solution)/shard_map/reduce_scatter | solution.py:152
  (103 shorter events, 28.2 us)
Async XLA Ops:
  7.2 1.9 copy-start
  7.2 834.1 %reduce-scatter.2.cloned.1.call-start = ((), (), s32[]{:S(2)}) async-start(), calls=%async_computation.1 | async-start | bytes 1622016 | tf_op jit(solution)/shard_map/reduce_scatter | solution.py:152
  15.5 11.9 %copy-start.5 = (s32[1,1,512]{2,1,0:T(1,128)S(1)}, s32[1,1,512]{2,1,0:T(1,128)}, u32[]{:S(2)}) copy-start(s32[1,1,512]{2,1,0:T(1,128)} %param.15) | copy-start | bytes 6148
  15.5 12.0 %copy-start.7 = (s32[4096]{0:T(1024)S(1)}, s32[4096]{0:T(1024)}, u32[]{:S(2)}) copy-start(s32[4096]{0:T(1024)} %param.17) | copy-start | bytes 49156
  15.6 21.9 %collective-permute-start.3 = (f32[2,16,1,256]{3,0,2,1:T(2,128)S(1)}, f32[2,16,1,256]{3,0,2,1:T(2,128)S(1)}, u32[]{:S(2)}, u32[]{:S(2)}) collective-permute-start(f32[2,16,1,256]{3,0,2,1:T(2,128)S(1)} %get-tuple-element.167), channel_id=1, source_target_pairs={{0,1},{1,2},{2,3},{3,4},{4,5},{5,6},{6,7},{8,9},{9,10},{10,11},{11... | collective-permute-start | bytes 98312 | tf_op jit(solution)/shard_map/ppermute | solution.py:20
  18.0 19.9 %collective-permute-start.2 = (f32[2,16,1,256]{3,0,2,1:T(2,128)S(1)}, f32[2,16,1,256]{3,0,2,1:T(2,128)S(1)}, u32[]{:S(2)}, u32[]{:S(2)}) collective-permute-start(f32[2,16,1,256]{3,0,2,1:T(2,128)S(1)} %get-tuple-element.168), channel_id=1, source_target_pairs={{1,0},{2,1},{3,2},{4,3},{5,4},{6,5},{7,6},{9,8},{10,9},{11,10},{12... | collective-permute-start | bytes 98312 | tf_op jit(solution)/shard_map/ppermute | solution.py:20
  19.3 18.8 %collective-permute-start.1 = (f32[2,1,16,256]{3,0,2,1:T(2,128)S(1)}, f32[2,1,16,256]{3,0,2,1:T(2,128)S(1)}, u32[]{:S(2)}, u32[]{:S(2)}) collective-permute-start(f32[2,1,16,256]{3,0,2,1:T(2,128)S(1)} %get-tuple-element.171), channel_id=1, source_target_pairs={{0,8},{8,16},{16,24},{1,9},{9,17},{17,25},{2,10},{10,18},{18,26},{... | collective-permute-start | bytes 98312 | tf_op jit(solution)/shard_map/ppermute | solution.py:20
  23.5 14.9 %collective-permute-start = (f32[2,1,16,256]{3,0,2,1:T(2,128)S(1)}, f32[2,1,16,256]{3,0,2,1:T(2,128)S(1)}, u32[]{:S(2)}, u32[]{:S(2)}) collective-permute-start(f32[2,1,16,256]{3,0,2,1:T(2,128)S(1)} %get-tuple-element.172), channel_id=1, source_target_pairs={{8,0},{16,8},{24,16},{9,1},{17,9},{25,17},{10,2},{18,10},{26,18},{... | collective-permute-start | bytes 98312 | tf_op jit(solution)/shard_map/ppermute | solution.py:20
  38.5 8.8 %copy-start.3 = (f32[16,16,256]{2,1,0:T(8,128)S(1)}, f32[16,16,256]{2,1,0:T(8,128)}, u32[]{:S(2)}) copy-start(f32[16,16,256]{2,1,0:T(8,128)} %param.14) | copy-start | bytes 786436
  38.5 8.8 %copy-start.4 = (f32[12,12,1,1]{1,0,3,2:T(8,128)S(1)}, f32[12,12,1,1]{1,0,3,2:T(8,128)}, u32[]{:S(2)}) copy-start(f32[12,12,1,1]{1,0,3,2:T(8,128)} %constant.222) | copy-start | bytes 1732
  55.2 41.3 %copy-start.6 = (f32[6,12]{1,0:T(8,128)S(1)}, f32[6,12]{1,0:T(8,128)}, u32[]{:S(2)}) copy-start(f32[6,12]{1,0:T(8,128)} %constant.211.clone) | copy-start | bytes 868
  73.7 24.1 %collective-permute-start.7 = (f32[2,16,1,256]{3,0,2,1:T(2,128)S(1)}, f32[2,16,1,256]{3,0,2,1:T(2,128)S(1)}, u32[]{:S(2)}, u32[]{:S(2)}) collective-permute-start(f32[2,16,1,256]{3,0,2,1:T(2,128)S(1)} %get-tuple-element.157), channel_id=1, source_target_pairs={{0,1},{1,2},{2,3},{3,4},{4,5},{5,6},{6,7},{8,9},{9,10},{10,11},{11... | collective-permute-start | bytes 98312 | tf_op jit(solution)/shard_map/ppermute | solution.py:20
  77.8 20.3 %collective-permute-start.6 = (f32[2,16,1,256]{3,0,2,1:T(2,128)S(1)}, f32[2,16,1,256]{3,0,2,1:T(2,128)S(1)}, u32[]{:S(2)}, u32[]{:S(2)}) collective-permute-start(f32[2,16,1,256]{3,0,2,1:T(2,128)S(1)} %get-tuple-element.158), channel_id=1, source_target_pairs={{1,0},{2,1},{3,2},{4,3},{5,4},{6,5},{7,6},{9,8},{10,9},{11,10},{12... | collective-permute-start | bytes 98312 | tf_op jit(solution)/shard_map/ppermute | solution.py:20
  79.1 19.3 %collective-permute-start.5 = (f32[2,1,16,256]{3,0,2,1:T(2,128)S(1)}, f32[2,1,16,256]{3,0,2,1:T(2,128)S(1)}, u32[]{:S(2)}, u32[]{:S(2)}) collective-permute-start(f32[2,1,16,256]{3,0,2,1:T(2,128)S(1)} %get-tuple-element.161), channel_id=1, source_target_pairs={{0,8},{8,16},{16,24},{1,9},{9,17},{17,25},{2,10},{10,18},{18,26},{... | collective-permute-start | bytes 98312 | tf_op jit(solution)/shard_map/ppermute | solution.py:20
  83.4 15.3 %collective-permute-start.4 = (f32[2,1,16,256]{3,0,2,1:T(2,128)S(1)}, f32[2,1,16,256]{3,0,2,1:T(2,128)S(1)}, u32[]{:S(2)}, u32[]{:S(2)}) collective-permute-start(f32[2,1,16,256]{3,0,2,1:T(2,128)S(1)} %get-tuple-element.162), channel_id=1, source_target_pairs={{8,0},{16,8},{24,16},{9,1},{17,9},{25,17},{10,2},{18,10},{26,18},{... | collective-permute-start | bytes 98312 | tf_op jit(solution)/shard_map/ppermute | solution.py:20
  107.5 30.5 %copy-start.8 = (s32[1,1,512]{2,1,0:T(1,128)S(1)}, s32[1,1,512]{2,1,0:T(1,128)}, u32[]{:S(2)}) copy-start(s32[1,1,512]{2,1,0:T(1,128)} %param.16) | copy-start | bytes 6148
  139.9 37.4 %copy-start.2 = (f32[4096,512]{1,0:T(8,128)S(1)}, f32[4096,512]{1,0:T(8,128)}, u32[]{:S(2)}) copy-start(f32[4096,512]{1,0:T(8,128)} %get-tuple-element.261) | copy-start | bytes 25165828 | tf_op jit(solution)/shard_map/while
  214.4 37.4 %copy-start.2 = (f32[4096,512]{1,0:T(8,128)S(1)}, f32[4096,512]{1,0:T(8,128)}, u32[]{:S(2)}) copy-start(f32[4096,512]{1,0:T(8,128)} %get-tuple-element.261) | copy-start | bytes 25165828 | tf_op jit(solution)/shard_map/while
  289.0 37.4 %copy-start.2 = (f32[4096,512]{1,0:T(8,128)S(1)}, f32[4096,512]{1,0:T(8,128)}, u32[]{:S(2)}) copy-start(f32[4096,512]{1,0:T(8,128)} %get-tuple-element.261) | copy-start | bytes 25165828 | tf_op jit(solution)/shard_map/while
  363.6 37.4 %copy-start.2 = (f32[4096,512]{1,0:T(8,128)S(1)}, f32[4096,512]{1,0:T(8,128)}, u32[]{:S(2)}) copy-start(f32[4096,512]{1,0:T(8,128)} %get-tuple-element.261) | copy-start | bytes 25165828 | tf_op jit(solution)/shard_map/while
  438.1 37.4 %copy-start.2 = (f32[4096,512]{1,0:T(8,128)S(1)}, f32[4096,512]{1,0:T(8,128)}, u32[]{:S(2)}) copy-start(f32[4096,512]{1,0:T(8,128)} %get-tuple-element.261) | copy-start | bytes 25165828 | tf_op jit(solution)/shard_map/while
  512.7 37.4 %copy-start.2 = (f32[4096,512]{1,0:T(8,128)S(1)}, f32[4096,512]{1,0:T(8,128)}, u32[]{:S(2)}) copy-start(f32[4096,512]{1,0:T(8,128)} %get-tuple-element.261) | copy-start | bytes 25165828 | tf_op jit(solution)/shard_map/while
  587.3 37.4 %copy-start.2 = (f32[4096,512]{1,0:T(8,128)S(1)}, f32[4096,512]{1,0:T(8,128)}, u32[]{:S(2)}) copy-start(f32[4096,512]{1,0:T(8,128)} %get-tuple-element.261) | copy-start | bytes 25165828 | tf_op jit(solution)/shard_map/while
  661.8 37.4 %copy-start.2 = (f32[4096,512]{1,0:T(8,128)S(1)}, f32[4096,512]{1,0:T(8,128)}, u32[]{:S(2)}) copy-start(f32[4096,512]{1,0:T(8,128)} %get-tuple-element.261) | copy-start | bytes 25165828 | tf_op jit(solution)/shard_map/while
  737.9 103.4 %copy-start.1 = (f32[12,16,16,256]{3,2,1,0:T(8,128)S(1)}, f32[12,16,16,256]{3,2,1,0:T(8,128)}, u32[]{:S(2)}) copy-start(f32[12,16,16,256]{3,2,1,0:T(8,128)} %param.13) | copy-start | bytes 9437188
Sparse Core Ops, SparseCore 0:
  738.0 103.2 reduce-scatter.1
where the time goes:
time: 849 us; the launch traced here: 848 us
  matrix products  605 us (71%)
  waiting for transfers between devices  97.6 us (11%)
  local copies, waits for them, and re-layouts  95.7 us (11%)
  starting transfers between devices  20.6 us (2%)
  between operations  14.5 us (2%)
    dot_general x8, matrix products, one_freq(): jnp.einsum('nm,cm->nc', jnp.sin(phase_angle), lower, precision=HIGH)  299 us
    dot_general x8, matrix products, one_freq(): jnp.einsum('nm,cm->nc', jnp.cos(phase_angle), upper, precision=HIGH)  284 us
    reduce_scatter x1, waiting for transfers between devices, per_device(): lax.psum_scatter(far_term(owner_dirs, slot_data, positions, scale), ('gx'...  97.6 us
    ppermute x8, starting transfers between devices, shifted(): return lax.ppermute(block, axis, route)  20.5 us
    reshape x1, local copies, waits for them, and re-layouts, per_device(): slots_two = jnp.take(incident_two.reshape(12, -1), cell_index, axis=1)  18.5 us
    reshape x1, local copies, waits for them, and re-layouts, per_device(): slots_one = jnp.take(incident_one.reshape(12, -1), cell_index, axis=1)  18.5 us
  transfers between devices with their start and end apart: 9, of which 1 were waited for; matrix products, arithmetic and copies ran while one was open for 4% of the time, Pallas kernels for 0%

commit v1 on v0

--- a/solution.py
+++ b/solution.py
@@ -4,6 +4,8 @@
 import jax.numpy as jnp
 import numpy as np
 from jax import lax
+from jax.experimental import pallas as pl
+from jax.experimental.pallas import tpu as pltpu
 from jax.sharding import PartitionSpec as P
 
 DIRS = 4096
@@ -90,36 +92,162 @@
     )
 
 
-def unit_vectors(direction_ids):
-    theta_count = DIRS // 64
-    theta = math.pi * ((direction_ids // 64).astype(jnp.float32) + 0.5) / theta_count
-    azimuth = 2.0 * math.pi * (direction_ids % 64).astype(jnp.float32) / 64.0
-    return jnp.stack(
-        [jnp.sin(theta) * jnp.cos(azimuth), jnp.sin(theta) * jnp.sin(azimuth), jnp.cos(theta)],
-        axis=1,
-    )
-
-
-def far_term(direction_ids, slot_data, positions, scale):
-    units = unit_vectors(direction_ids)
-    projected = jnp.dot(units, positions, precision=HIGH)
-    first = slot_data[0:6]
-    second = slot_data[6:12]
-
-    def one_freq(f_index):
-        omega = 2.0 * math.pi * (f_index + 1.0) / 64.0
-        real_part = first * jnp.cos(omega) + second * jnp.cos(2.0 * omega)
-        imag_part = -(first * jnp.sin(omega) + second * jnp.sin(2.0 * omega))
-        phase_angle = 2.0 * omega * projected
-        upper = jnp.concatenate([real_part, imag_part], axis=0)
-        lower = jnp.concatenate([-imag_part, real_part], axis=0)
-        return jnp.einsum("nm,cm->nc", jnp.cos(phase_angle), upper, precision=HIGH) + jnp.einsum(
-            "nm,cm->nc", jnp.sin(phase_angle), lower, precision=HIGH
+def trig_coefficients():
+    nodes = np.cos(np.pi * (np.arange(64) + 0.5) / 64)
+    square = 0.125 * (nodes + 1.0)
+    turn = np.sqrt(square)
+    cos_fit = np.polynomial.chebyshev.Chebyshev.fit(
+        square, np.cos(2 * np.pi * turn), 6, domain=[0.0, 0.25]
+    )
+    sin_fit = np.polynomial.chebyshev.Chebyshev.fit(
+        square, np.sin(2 * np.pi * turn) / turn, 6, domain=[0.0, 0.25]
+    )
+    to_poly = lambda fit: [float(v) for v in fit.convert(kind=np.polynomial.Polynomial).coef]
+    return to_poly(cos_fit), to_poly(sin_fit)
+
+
+def horner(coefficients, at):
+    total = jnp.full_like(at, coefficients[-1])
+    for value in coefficients[-2::-1]:
+        total = total * at + value
+    return total
+
+
+def cos_sin_turns(turns):
+    cos_poly, sin_poly = trig_coefficients()
+    rest = turns - jnp.round(turns)
+    square = rest * rest
+    return horner(cos_poly, square), rest * horner(sin_poly, square)
+
+
+def split_two(values):
+    high = values.astype(jnp.bfloat16)
+    low = (values - high.astype(jnp.float32)).astype(jnp.bfloat16)
+    return high, low
+
+
+def output_weights(scale):
+    weights = np.zeros((FREQ, 2, 2, 16, FREQ * 12))
+    for f in range(FREQ):
+        for t in (1, 2):
+            w = 2.0 * math.pi * (f + 1) / 64.0 * t
+            for c in range(6):
+                row = 8 * (t - 1) + c
+                weights[f, 0, :, row, 12 * f + c] = math.cos(w)
+                weights[f, 1, :, row, 12 * f + c] = math.sin(w)
+                weights[f, 0, :, row, 12 * f + 6 + c] = -math.sin(w)
+                weights[f, 1, :, row, 12 * f + 6 + c] = math.cos(w)
+    return (weights * scale).reshape(2 * FREQ, 32, 12 * FREQ).astype(np.float32)
+
+
+CHUNK = 256
+GROUP = 32
+
+
+def far_kernel(gathered, dirs, weights, out, packed, totals, counts_v, counts_s, sem):
+    devices, _, slots = gathered.shape
+    rows = dirs.shape[1]
+    flags = gathered[:, 15, :]
+    live = jnp.sum(flags, axis=1, keepdims=True).astype(jnp.int32)
+    counts_v[...] = jnp.broadcast_to(live, counts_v.shape)
+    copy = pltpu.make_async_copy(counts_v, counts_s, sem)
+    copy.start()
+
+    ids = dirs[...]
+    theta = (ids // 64).astype(jnp.float32) * (1.0 / 128.0) + 1.0 / 256.0
+    azimuth = (ids % 64).astype(jnp.float32) * (1.0 / 64.0)
+    cos_t, sin_t = cos_sin_turns(theta)
+    cos_a, sin_a = cos_sin_turns(azimuth)
+    units = jnp.concatenate([sin_t * cos_a, sin_t * sin_a, cos_t], axis=0) * (1.0 / 32.0)
+    first = units.astype(jnp.bfloat16).astype(jnp.float32)
+    second = (units - first).astype(jnp.bfloat16).astype(jnp.float32)
+    third = units - first - second
+    stack = jnp.concatenate(
+        [first, second, third, first, second, jnp.zeros((rows - 15, rows), jnp.float32)], axis=0
+    )
+    unit_cols = stack.T[:, :16].astype(jnp.bfloat16)
+    totals[...] = jnp.zeros_like(totals)
+    copy.wait()
+
+    lane = lax.broadcasted_iota(jnp.int32, (16, 128), 1)
+    pad = jnp.zeros((16, 128), jnp.float32)
+
+    def pack(d, offset):
+        base = pl.multiple_of((offset >> 7) << 7, 128)
+        shift = offset & 127
+        block = pltpu.roll(jnp.concatenate([gathered[d], pad], axis=1), shift, 1)
+        packed[:, pl.ds(base, 128)] = jnp.where(
+            lane < shift, packed[:, pl.ds(base, 128)], block[:, :128]
         )
-
-    per_freq = lax.map(one_freq, jnp.arange(FREQ, dtype=jnp.float32))
-    rows_here = direction_ids.shape[0]
-    return jnp.transpose(per_freq, (1, 0, 2)).reshape(rows_here, FREQ * 12) * scale
+        packed[:, pl.ds(base + 128, slots)] = block[:, 128:]
+        packed[:, pl.ds(base + 128 + slots, CHUNK)] = jnp.zeros((16, CHUNK), jnp.float32)
+        return offset + counts_s[d, 0]
+
+    total = lax.fori_loop(0, devices, pack, jnp.int32(0))
+
+    def chunk_step(index, carry):
+        block = packed[:, pl.ds(pl.multiple_of(index * CHUNK, CHUNK), CHUNK)]
+        high, low = split_two(block)
+        currents = jnp.concatenate([high, low], axis=0)
+        place = jnp.concatenate([block[6:8], block[14:15]], axis=0)
+        place_high = place.astype(jnp.bfloat16).astype(jnp.float32)
+        place_low = place - place_high
+        places = jnp.concatenate(
+            [place_high] * 3 + [place_low] * 2 + [jnp.zeros((1, CHUNK), jnp.float32)], axis=0
+        ).astype(jnp.bfloat16)
+        turns = jnp.dot(unit_cols, places, preferred_element_type=jnp.float32)
+        for g in range(rows // GROUP):
+            cos_one, sin_one = cos_sin_turns(turns[g * GROUP : (g + 1) * GROUP])
+            double = 2.0 * cos_one
+            cos_old, sin_old = jnp.ones_like(cos_one), jnp.zeros_like(sin_one)
+            cos_now, sin_now = cos_one, sin_one
+            highs, lows = [], []
+            for f in range(FREQ):
+                for value in (cos_now, sin_now):
+                    upper, lower = split_two(value)
+                    highs.append(upper)
+                    lows.append(lower)
+                if f < FREQ - 1:
+                    cos_now, cos_old = double * cos_now - cos_old, cos_now
+                    sin_now, sin_old = double * sin_now - sin_old, sin_now
+            span = 2 * FREQ * GROUP
+            both = jnp.concatenate(highs + lows, axis=0)
+            product = lax.dot_general(
+                both, currents, (((1,), (1,)), ((), ())), preferred_element_type=jnp.float32
+            )
+            totals[pl.ds(g * span, span), :] += product[:span] + product[span:]
+        return carry
+
+    lax.fori_loop(0, (total + CHUNK - 1) >> 8, chunk_step, 0)
+
+    for g in range(rows // GROUP):
+        result = jnp.zeros((GROUP, 12 * FREQ), jnp.float32)
+        for k in range(2 * FREQ):
+            part = totals[pl.ds((g * 2 * FREQ + k) * GROUP, GROUP), :]
+            result += jnp.dot(
+                part, weights[k], precision=HIGH, preferred_element_type=jnp.float32
+            )
+        out[pl.ds(g * GROUP, GROUP), :] = result
+
+
+def far_field_of(gathered, own_dirs, scale):
+    devices, _, slots = gathered.shape
+    rows = own_dirs.shape[1]
+    vmem = pl.BlockSpec(memory_space=pltpu.VMEM)
+    return pl.pallas_call(
+        far_kernel,
+        out_shape=jax.ShapeDtypeStruct((rows, 12 * FREQ), jnp.float32),
+        in_specs=[vmem] * 3,
+        out_specs=vmem,
+        scratch_shapes=[
+            pltpu.VMEM((16, devices * slots + 128 + CHUNK), jnp.float32),
+            pltpu.VMEM((2 * FREQ * rows, 32), jnp.float32),
+            pltpu.VMEM((devices, 128), jnp.int32),
+            pltpu.SMEM((devices, 128), jnp.int32),
+            pltpu.SemaphoreType.DMA,
+        ],
+        compiler_params=pltpu.CompilerParams(vmem_limit_bytes=48 * 1024 * 1024),
+    )(gathered, own_dirs, jnp.asarray(output_weights(scale)))
 
 
 def per_device(pulses_in, node_loss, surface_cells, surface_normal, owner_dirs):
@@ -149,12 +277,15 @@
         ]
     )
     scale = 1.0 / math.sqrt(size_x * size_y * slot_count)
-    far_field = lax.psum_scatter(
-        far_term(owner_dirs, slot_data, positions, scale),
-        ("gx", "gy"),
-        scatter_dimension=0,
-        tiled=True,
-    )
+    live = (codes > 0).astype(jnp.float32)[None]
+    mine = jnp.concatenate(
+        [slot_data[0:6], positions[0:2], slot_data[6:12], positions[2:3], live], axis=0
+    )
+    gathered = lax.all_gather(mine, ("gx", "gy"))
+    rows = owner_dirs.shape[0] // (size_x * size_y)
+    own = lax.axis_index("gx") * size_y + lax.axis_index("gy")
+    own_dirs = lax.dynamic_slice(owner_dirs, (own * rows,), (rows,))[None]
+    far_field = far_field_of(gathered, own_dirs, scale)
     return (incident_two, far_field)
 
 

time: 849 us -> 234 us (0.28)
  matrix products: 605 us -> 12.8 us
  waiting for transfers between devices: 97.6 us -> 53.6 us
  Pallas kernels: 0 us -> 38.2 us
    dot_general x17 -> x0, matrix products: 592 us -> none  [the longest x8 299 us: one_freq(): jnp.einsum('nm,cm->nc', jnp.sin(phase_angle), lower, precision=HIGH)]
    reduce_scatter x1 -> x0, waiting for transfers between devices: 97.6 us -> none  [per_device(): lax.psum_scatter(far_term(owner_dirs, slot_data, positions, scale), ('gx'...]
    all_gather x0 -> x1, waiting for transfers between devices: none -> 53.5 us  [per_device(): gathered = lax.all_gather(mine, ('gx', 'gy'))]
    pallas_call x0 -> x1, Pallas kernels: none -> 38.2 us  [far_field_of(): pl.pallas_call(far_kernel, out_shape=jax.ShapeDtypeStruct((rows, 12 * FRE...]
  transfers between devices with their start and end apart: 9 -> 9, of which waited for: 1 -> 1; matrix products, arithmetic and copies ran while one was open for 4% -> 10% of each run, Pallas kernels for 0% -> 0%
where the time goes in v1:
time: 234 us; the launch traced here: 236 us
  local copies, waits for them, and re-layouts  93.2 us (40%)
  waiting for transfers between devices  53.6 us (23%)
  Pallas kernels  38.2 us (16%)
  starting transfers between devices  20.6 us (9%)
  between operations  14.5 us (6%)
  matrix products  12.8 us (5%)
  other arithmetic  3.65 us (2%)
    all_gather x1, waiting for transfers between devices, per_device(): gathered = lax.all_gather(mine, ('gx', 'gy'))  53.5 us
    pallas_call x1, Pallas kernels, far_field_of(): pl.pallas_call(far_kernel, out_shape=jax.ShapeDtypeStruct((rows, 12 * FRE...  38.2 us
    ppermute x8, starting transfers between devices, shifted(): return lax.ppermute(block, axis, route)  20.5 us
    reshape x1, local copies, waits for them, and re-layouts, per_device(): slots_one = jnp.take(incident_one.reshape(12, -1), cell_index, axis=1)  18.5 us
    reshape x1, local copies, waits for them, and re-layouts, per_device(): slots_two = jnp.take(incident_two.reshape(12, -1), cell_index, axis=1)  18.5 us
    concatenate x2, local copies, waits for them, and re-layouts, connect_tile(): jnp.concatenate([plus_x, minus_x, plus_y, minus_y, plus_z, minus_z], axis=0)  14.7 us
    dot_general x2, matrix products, scatter_node(): jnp.einsum('kl,lxyz->kxyz', scatter_table, incident, precision=HIGH)  11.9 us
    gather x1, local copies, waits for them, and re-layouts, per_device(): slots_two = jnp.take(incident_two.reshape(12, -1), cell_index, axis=1)  11.6 us
  transfers between devices with their start and end apart: 9, of which 1 were waited for; matrix products, arithmetic and copies ran while one was open for 10% of the time, Pallas kernels for 0%

profile of v1, /device:TPU:0, one launch (start us, length us, event | category | flops | bytes accessed | tf_op | source)
XLA Modules:
  0.0 236.5 jit_solution(12060815706651252639)
XLA Ops:
  7.2 1.8 copy-done
  9.1 6.5 %fusion.2 = f32[12,16,16,256]{3,0,2,1:T(8,128)S(1)} fusion(f32[12,12,1,1]{1,0,3,2:T(8,128)} %constant.135, f32[12,16,16,256]{3,2,1,0:T(8,128)S(1)} %copy-done, f32[16,16,256]{2,1,0:T(8,128)} %param.13), kind=kOutput, calls=%fused_computation.5 | convolution fusion | flops 114032640 | bytes 6554176 | tf_op jit(solution)/shard_map/kl,lxyz->kxyz/dot_general | solution.py:53
  15.6 2.4 collective-permute-start.3
  18.0 1.3 collective-permute-start.2
  19.3 4.2 %collective-permute-start.1 = (f32[2,1,16,256]{3,0,2,1:T(2,128)S(1)}, f32[2,1,16,256]{3,0,2,1:T(2,128)S(1)}, u32[]{:S(2)}, u32[]{:S(2)}) collective-permute-start(f32[2,1,16,256]{3,0,2,1:T(2,128)S(1)} %get-tuple-element.32), channel_id=1, source_target_pairs={{0,8},{8,16},{16,24},{1,9},{9,17},{17,25},{2,10},{10,18},{18,26},{... | collective-permute-start | bytes 98312 | tf_op jit(solution)/shard_map/ppermute | solution.py:22
  23.5 1.5 collective-permute-start
  25.4 1.3 fusion.42
  26.7 0.7 fusion.38
  27.8 0.6 concatenate.50
  29.7 7.4 %concatenate.51 = f32[12,16,16,256]{3,0,2,1:T(8,128)} concatenate(f32[2,16,16,256]{3,0,2,1:T(2,128)S(1)} %pad_maximum_fusion, f32[2,16,16,256]{3,0,2,1:T(2,128)S(1)} %pad_maximum_fusion.1, f32[2,16,16,256]{3,0,2,1:T(2,128)S(1)} %pad_maximum_fusion.2, f32[2,16,16,256]{3,0,2,1:T(2,128)S(1)} %pad_maximum_fusion.3, f32[2,16,16,256]{3,0,2,1:T(2,128)S(1)} %concatenate.49, ...), dimensions={0} | concatenate | bytes 6291456 | tf_op jit(solution)/shard_map/concatenate | solution.py:68
  37.1 5.5 %multiply_bitcast_fusion = f32[12,16,16,256]{3,0,2,1:T(8,128)S(1)} fusion(f32[12,16,16,256]{3,0,2,1:T(8,128)} %concatenate.51, f32[12,12,1,1]{1,0,3,2:T(8,128)S(1)} %copy-done.6, f32[16,16,256]{2,1,0:T(8,128)S(1)} %copy-done.5), kind=kOutput, calls=%fused_computation.4 | convolution fusion | flops 114032640 | bytes 6554176 | tf_op jit(solution)/shard_map/kl,lxyz->kxyz/dot_general | solution.py:53
  43.0 1.3 fusion.37
  44.3 0.7 fusion.33
  45.0 18.5 %copy.23 = f32[12,16,16,256]{0,3,2,1:T(8,128)} copy(f32[12,16,16,256]{3,0,2,1:T(8,128)} %concatenate.51) | data formatting | bytes 6291456 | tf_op jit(solution)/shard_map/reshape | solution.py:264
  63.5 4.1 %collective-permute-start.7 = (f32[2,16,1,256]{3,0,2,1:T(2,128)S(1)}, f32[2,16,1,256]{3,0,2,1:T(2,128)S(1)}, u32[]{:S(2)}, u32[]{:S(2)}) collective-permute-start(f32[2,16,1,256]{3,0,2,1:T(2,128)S(1)} %get-tuple-element.18), channel_id=1, source_target_pairs={{0,1},{1,2},{2,3},{3,4},{4,5},{5,6},{6,7},{8,9},{9,10},{10,11},{11... | collective-permute-start | bytes 98312 | tf_op jit(solution)/shard_map/ppermute | solution.py:22
  67.7 1.3 collective-permute-start.6
  69.0 4.3 %collective-permute-start.5 = (f32[2,1,16,256]{3,0,2,1:T(2,128)S(1)}, f32[2,1,16,256]{3,0,2,1:T(2,128)S(1)}, u32[]{:S(2)}, u32[]{:S(2)}) collective-permute-start(f32[2,1,16,256]{3,0,2,1:T(2,128)S(1)} %get-tuple-element.22), channel_id=1, source_target_pairs={{0,8},{8,16},{16,24},{1,9},{9,17},{17,25},{2,10},{10,18},{18,26},{... | collective-permute-start | bytes 98312 | tf_op jit(solution)/shard_map/ppermute | solution.py:22
  73.2 1.5 collective-permute-start.4
  74.7 11.6 %gather_fusion = f32[512,12]{1,0:T(8,128)S(1)} fusion(f32[12,65536]{0,1:T(8,128)} %bitcast.72, s32[1024]{0:T(1024)S(1)} %pad_clamp_fusion), kind=kCustom, calls=%fused_computation.clone | custom fusion | bytes 51200 | tf_op jit(solution)/shard_map/jit(_take)/gather | solution.py:264
  86.3 0.4 fusion.7
  87.0 0.6 concatenate.57
  88.6 1.4 pad_maximum_fusion.4
  90.0 7.4 %concatenate.58 = f32[12,16,16,256]{3,0,2,1:T(8,128)} concatenate(f32[2,16,16,256]{3,0,2,1:T(2,128)S(1)} %pad_maximum_fusion.4, f32[2,16,16,256]{3,0,2,1:T(2,128)S(1)} %pad_maximum_fusion.5, f32[2,16,16,256]{3,0,2,1:T(2,128)S(1)} %pad_maximum_fusion.6, f32[2,16,16,256]{3,0,2,1:T(2,128)S(1)} %pad_maximum_fusion.7, f32[2,16,16,256]{3,0,2,1:T(2,128)S(1)} %concatenate.56, ...), dimensions={0} | concatenate | bytes 6291456 | tf_op jit(solution)/shard_map/concatenate | solution.py:68
  97.3 18.5 %copy.24 = f32[12,16,16,256]{0,3,2,1:T(8,128)} copy(f32[12,16,16,256]{3,0,2,1:T(8,128)} %concatenate.58) | data formatting | bytes 6291456 | tf_op jit(solution)/shard_map/reshape | solution.py:265
  115.8 11.6 %gather_fusion.1 = f32[512,12]{1,0:T(8,128)S(1)} fusion(f32[12,65536]{0,1:T(8,128)} %bitcast.73, s32[1024]{0:T(1024)S(1)} %pad_clamp_fusion), kind=kCustom, calls=%fused_computation.1.clone | custom fusion | bytes 51200 | tf_op jit(solution)/shard_map/jit(_take)/gather | solution.py:265
  128.0 1.3 concatenate.59
  129.3 0.9 dynamic-slice_bitcast_fusion.dirs
  130.2 5.7 %copy.20 = f32[12,16,16,256]{3,2,1,0:T(8,128)} copy(f32[12,16,16,256]{3,0,2,1:T(8,128)} %concatenate.58) | data formatting | bytes 6291456
  136.0 53.5 %all-gather.3.cloned.1.call-done = f32[512,512]{1,0:T(8,128)} async-done(((f32[16,512]{1,0:T(8,128)}), f32[512,512]{1,0:T(8,128)}) %all-gather.3.cloned.1.call-update) | async-done | bytes 1048592 | tf_op jit(solution)/shard_map/all_gather | solution.py:284
  189.5 1.2 copy-done.2
  190.7 38.2 %shard_map.113 = f32[128,96]{1,0:T(8,128)S(1)} custom-call(f32[32,16,512]{2,1,0:T(8,128)S(1)} %bitcast.71, s32[1,128]{1,0:T(1,128)S(1)} %dynamic-slice_bitcast_fusion.dirs, f32[16,32,96]{2,1,0:T(8,128)S(1)} %copy-done.3), custom_call_target="tpu_custom_call" | custom-call | tf_op jit(solution)/shard_map/pallas_call | solution.py:237
  228.9 0.7 copy.21
  (55 shorter events, 4.2 us)
Async XLA Ops:
  7.2 1.9 copy-start
  7.2 182.3 %all-gather.3.cloned.1.call-start = ((), (), s32[]{:S(2)}) async-start(), calls=%async_computation | async-start | bytes 1081344 | tf_op jit(solution)/shard_map/all_gather | solution.py:284
  15.5 11.9 %copy-start.7 = (s32[1,1,512]{2,1,0:T(1,128)S(1)}, s32[1,1,512]{2,1,0:T(1,128)}, u32[]{:S(2)}) copy-start(s32[1,1,512]{2,1,0:T(1,128)} %param.14) | copy-start | bytes 6148
  15.5 11.9 %copy-start.8 = (s32[1,1,512]{2,1,0:T(1,128)S(1)}, s32[1,1,512]{2,1,0:T(1,128)}, u32[]{:S(2)}) copy-start(s32[1,1,512]{2,1,0:T(1,128)} %param.15) | copy-start | bytes 6148
  15.6 12.8 %collective-permute-start.3 = (f32[2,16,1,256]{3,0,2,1:T(2,128)S(1)}, f32[2,16,1,256]{3,0,2,1:T(2,128)S(1)}, u32[]{:S(2)}, u32[]{:S(2)}) collective-permute-start(f32[2,16,1,256]{3,0,2,1:T(2,128)S(1)} %get-tuple-element.28), channel_id=1, source_target_pairs={{0,1},{1,2},{2,3},{3,4},{4,5},{5,6},{6,7},{8,9},{9,10},{10,11},{11... | collective-permute-start | bytes 98312 | tf_op jit(solution)/shard_map/ppermute | solution.py:22
  18.0 10.7 %collective-permute-start.2 = (f32[2,16,1,256]{3,0,2,1:T(2,128)S(1)}, f32[2,16,1,256]{3,0,2,1:T(2,128)S(1)}, u32[]{:S(2)}, u32[]{:S(2)}) collective-permute-start(f32[2,16,1,256]{3,0,2,1:T(2,128)S(1)} %get-tuple-element.29), channel_id=1, source_target_pairs={{1,0},{2,1},{3,2},{4,3},{5,4},{6,5},{7,6},{9,8},{10,9},{11,10},{12... | collective-permute-start | bytes 98312 | tf_op jit(solution)/shard_map/ppermute | solution.py:22
  19.3 9.7 %collective-permute-start.1 = (f32[2,1,16,256]{3,0,2,1:T(2,128)S(1)}, f32[2,1,16,256]{3,0,2,1:T(2,128)S(1)}, u32[]{:S(2)}, u32[]{:S(2)}) collective-permute-start(f32[2,1,16,256]{3,0,2,1:T(2,128)S(1)} %get-tuple-element.32), channel_id=1, source_target_pairs={{0,8},{8,16},{16,24},{1,9},{9,17},{17,25},{2,10},{10,18},{18,26},{... | collective-permute-start | bytes 98312 | tf_op jit(solution)/shard_map/ppermute | solution.py:22
  23.5 5.8 %collective-permute-start = (f32[2,1,16,256]{3,0,2,1:T(2,128)S(1)}, f32[2,1,16,256]{3,0,2,1:T(2,128)S(1)}, u32[]{:S(2)}, u32[]{:S(2)}) collective-permute-start(f32[2,1,16,256]{3,0,2,1:T(2,128)S(1)} %get-tuple-element.33), channel_id=1, source_target_pairs={{8,0},{16,8},{24,16},{9,1},{17,9},{25,17},{10,2},{18,10},{26,18},{... | collective-permute-start | bytes 98312 | tf_op jit(solution)/shard_map/ppermute | solution.py:22
  27.5 1.9 copy-start.4
  29.3 7.7 %copy-start.5 = (f32[16,16,256]{2,1,0:T(8,128)S(1)}, f32[16,16,256]{2,1,0:T(8,128)}, u32[]{:S(2)}) copy-start(f32[16,16,256]{2,1,0:T(8,128)} %param.13) | copy-start | bytes 786436
  29.4 7.7 %copy-start.6 = (f32[12,12,1,1]{1,0,3,2:T(8,128)S(1)}, f32[12,12,1,1]{1,0,3,2:T(8,128)}, u32[]{:S(2)}) copy-start(f32[12,12,1,1]{1,0,3,2:T(8,128)} %constant.135) | copy-start | bytes 1732
  45.0 41.3 %copy-start.9 = (f32[6,12]{1,0:T(8,128)S(1)}, f32[6,12]{1,0:T(8,128)}, u32[]{:S(2)}) copy-start(f32[6,12]{1,0:T(8,128)} %constant.123.clone) | copy-start | bytes 868
  63.5 24.1 %collective-permute-start.7 = (f32[2,16,1,256]{3,0,2,1:T(2,128)S(1)}, f32[2,16,1,256]{3,0,2,1:T(2,128)S(1)}, u32[]{:S(2)}, u32[]{:S(2)}) collective-permute-start(f32[2,16,1,256]{3,0,2,1:T(2,128)S(1)} %get-tuple-element.18), channel_id=1, source_target_pairs={{0,1},{1,2},{2,3},{3,4},{4,5},{5,6},{6,7},{8,9},{9,10},{10,11},{11... | collective-permute-start | bytes 98312 | tf_op jit(solution)/shard_map/ppermute | solution.py:22
  67.7 20.3 %collective-permute-start.6 = (f32[2,16,1,256]{3,0,2,1:T(2,128)S(1)}, f32[2,16,1,256]{3,0,2,1:T(2,128)S(1)}, u32[]{:S(2)}, u32[]{:S(2)}) collective-permute-start(f32[2,16,1,256]{3,0,2,1:T(2,128)S(1)} %get-tuple-element.19), channel_id=1, source_target_pairs={{1,0},{2,1},{3,2},{4,3},{5,4},{6,5},{7,6},{9,8},{10,9},{11,10},{12... | collective-permute-start | bytes 98312 | tf_op jit(solution)/shard_map/ppermute | solution.py:22
  69.0 19.3 %collective-permute-start.5 = (f32[2,1,16,256]{3,0,2,1:T(2,128)S(1)}, f32[2,1,16,256]{3,0,2,1:T(2,128)S(1)}, u32[]{:S(2)}, u32[]{:S(2)}) collective-permute-start(f32[2,1,16,256]{3,0,2,1:T(2,128)S(1)} %get-tuple-element.22), channel_id=1, source_target_pairs={{0,8},{8,16},{16,24},{1,9},{9,17},{17,25},{2,10},{10,18},{18,26},{... | collective-permute-start | bytes 98312 | tf_op jit(solution)/shard_map/ppermute | solution.py:22
  73.2 15.3 %collective-permute-start.4 = (f32[2,1,16,256]{3,0,2,1:T(2,128)S(1)}, f32[2,1,16,256]{3,0,2,1:T(2,128)S(1)}, u32[]{:S(2)}, u32[]{:S(2)}) collective-permute-start(f32[2,1,16,256]{3,0,2,1:T(2,128)S(1)} %get-tuple-element.23), channel_id=1, source_target_pairs={{8,0},{16,8},{24,16},{9,1},{17,9},{25,17},{10,2},{18,10},{26,18},{... | collective-permute-start | bytes 98312 | tf_op jit(solution)/shard_map/ppermute | solution.py:22
  115.8 73.7 %copy-start.3 = (f32[16,32,96]{2,1,0:T(8,128)S(1)}, f32[16,32,96]{2,1,0:T(8,128)}, u32[]{:S(2)}) copy-start(f32[16,32,96]{2,1,0:T(8,128)} %constant.124.clone.weights) | copy-start | bytes 589828
  129.3 100.3 %copy-start.1 = (f32[12,16,16,256]{3,2,1,0:T(8,128)S(1)}, f32[12,16,16,256]{3,2,1,0:T(8,128)}, u32[]{:S(2)}) copy-start(f32[12,16,16,256]{3,2,1,0:T(8,128)} %param.12) | copy-start | bytes 9437188
  189.5 1.2 copy-start.2
Sparse Core Ops, SparseCore 0:
  129.4 60.0 all-gather.2
